TPU v7x, 32 devices: a whole 2x2x4 slice. The times are simulated.
32 devices in a mesh: rep: 4 (over y, core), fsdp: 8 (over z, x).
Axes of the slice: x: 2, y: 2, z: 4, core: 2. Of those that a mesh axis runs over, the one named last changes fastest.
Arguments:
- codes: int32 [4, 4194304], P('rep', 'fsdp'), may hold values from 0 to 15
- scales: float32 [4, 65536], P('rep', 'fsdp'), may hold values from 0.02 to 0.3
- base: float32 [4194304], P('fsdp'), may hold values from -6 to 6
- momentum: float32 [4194304], P('fsdp'), may hold values from -3 to 3
- inputs: bfloat16 [4, 1024, 8192], P('rep', 'fsdp'), may hold values from -30 to 30
- gain: bfloat16 [4, 8192], P('rep', 'fsdp'), may hold values from 0.099609375 to 1.8984375
- cotangent: bfloat16 [4, 1024, 512], P('rep', 'fsdp'), may hold values from -0.5 to 0.5
Outputs:
- new_base: float32 [4194304], P('fsdp')
- new_momentum: float32 [4194304], P('fsdp')
- keys: bfloat16 [4, 1024, 512], P('rep', 'fsdp')
- grad_weight: float32 [4, 8192, 512], P('rep', 'fsdp')
- grad_gain: float32 [4, 8192], P('rep', 'fsdp')
Inputs may be any that keep to these rules, and one draw needn't show every extreme that they name: `codes`: each entry is one 4-bit code.
All inputs are finite; a program needn't handle non-finite values.
Results may differ from a plain program's by a relative error of at most 0.015.
Values may be sent and summed in bfloat16 or wider, within the bound.
No kernel may reach another device: no remote copies, remote signals or barrier semaphores. Data moves between devices by JAX's collectives and lax.ppermute only.
A program may use at most 64 MiB of HBM per device.

v0:
```python
import jax
import jax.numpy as jnp
from jax import lax
from jax.sharding import PartitionSpec as P

D = 8192
BLOCK = 64


outer_rate = 0.7
momentum_decay = 0.9


def shards(codes, scales, base, momentum, inputs, gain, cotangent):
    decoded = (codes[0] - 8).astype(jnp.float32) * jnp.repeat(scales[0], BLOCK)
    replicas = lax.axis_size("rep")
    average = lax.psum(decoded.astype(jnp.bfloat16), "rep").astype(jnp.float32) / replicas
    new_momentum = momentum_decay * momentum + average
    new_base = base - outer_rate * (average + momentum_decay * new_momentum)
    activations = inputs[0]
    upstream = cotangent[0]
    own_gain = gain[0]
    own_rows = own_gain.shape[0]
    tok_rows = activations.shape[0]
    key_width = upstream.shape[1]
    own_weight = (new_base.reshape(own_rows, key_width) * D ** (-0.5)).astype(jnp.bfloat16)
    contract_last = (((1,), (1,)), ((), ()))
    wide = activations.astype(jnp.float32)
    inv_rms = lax.rsqrt(jnp.mean(wide * wide, axis=1) + 1e-05)
    every_scale = lax.all_gather(inv_rms, "fsdp", axis=0, tiled=True)
    columns = lax.all_to_all(activations, "fsdp", split_axis=1, concat_axis=0, tiled=True)
    every_upstream = lax.all_gather(upstream, "fsdp", axis=0, tiled=True)
    scaled = columns.astype(jnp.float32) * every_scale[:, None]
    normed_cols = (scaled * own_gain.astype(jnp.float32)).astype(jnp.bfloat16)
    grad_rows = lax.dot_general(
        normed_cols, every_upstream, (((0,), (0,)), ((), ())), preferred_element_type=jnp.float32
    )
    back = lax.dot_general(
        every_upstream, own_weight, contract_last, preferred_element_type=jnp.float32
    )
    grad_total = jnp.sum(back * scaled, axis=0)
    weight_piece = lax.all_gather(own_weight, "fsdp", axis=0, tiled=True)
    gain_piece = lax.all_gather(own_gain, "fsdp", axis=0, tiled=True)
    count = weight_piece.shape[0]
    blocks = count // own_rows
    normed = (wide * inv_rms[:, None] * gain_piece.astype(jnp.float32)).astype(jnp.bfloat16)
    partial_value = jnp.einsum(
        "tgr,grk->gtk",
        normed.reshape(tok_rows, blocks, own_rows),
        weight_piece.reshape(blocks, own_rows, key_width),
        preferred_element_type=jnp.float32,
    )
    partial_value = lax.optimization_barrier(partial_value.astype(jnp.bfloat16)).astype(jnp.float32)
    key_total = jnp.sum(partial_value, axis=0)
    return (
        new_base,
        new_momentum,
        key_total.astype(jnp.bfloat16)[None],
        grad_rows[None],
        grad_total[None],
    )


def solution(mesh):
    placed = (
        P("rep", "fsdp"),
        P("rep", "fsdp"),
        P("fsdp"),
        P("fsdp"),
        P("rep", "fsdp", None),
        P("rep", "fsdp"),
        P("rep", "fsdp", None),
    )
    return jax.shard_map(
        shards,
        mesh=mesh,
        in_specs=placed,
        out_specs=(
            P("fsdp"),
            P("fsdp"),
            P("rep", "fsdp", None),
            P("rep", "fsdp", None),
            P("rep", "fsdp"),
        ),
        check_vma=False,
    )
```

profile of v0, /device:TPU:0, one launch (start us, length us, event | category | flops | bytes accessed | tf_op | source)
XLA Modules:
  0.0 246.8 jit_solution(11042220870014154002)
XLA Ops:
  8.0 0.0 all-reduce.2.cloned.1.call-start
  8.1 4.7 %add_convert_fusion = f32[1,524288]{1,0:T(1,128)} fusion(s32[1,524288]{1,0:T(1,128)} %param.7), kind=kLoop, calls=%fused_computation.14 | loop fusion | flops 1048576 | bytes 4194304 | tf_op jit(solution)/shard_map/convert_element_type | solution.py:15
  12.7 0.0 copy-done.4
  12.7 2.5 %broadcast_in_dim.16 = f32[8192,64]{1,0:T(8,128)} broadcast(f32[8192]{0:T(1024)S(1)} %bitcast.39), dimensions={0} | broadcast | bytes 2129920 | tf_op jit(solution)/shard_map/broadcast_in_dim | solution.py:15
  15.3 3.3 %reshape.51 = f32[524288]{0:T(1024)S(1)} reshape(f32[8192,64]{1,0:T(8,128)} %broadcast_in_dim.16) | data formatting | bytes 4194304 | tf_op jit(solution)/shard_map/reshape | solution.py:15
  18.5 2.7 %multiply_convert_fusion.4 = bf16[524288]{0:T(1024)(128)(2,1)} fusion(f32[524288]{0:T(1024)} %bitcast.37, f32[524288]{0:T(1024)S(1)} %reshape.51), kind=kLoop, calls=%fused_computation.13 | loop fusion | flops 1048576 | bytes 5242880 | tf_op jit(solution)/shard_map/convert_element_type | solution.py:17
  21.3 0.0 all-reduce.2.cloned.1.call-update
  21.3 0.0 all-gather.8.cloned.1.call-start
  21.4 0.5 all-gather.8.cloned.1.call-update
  21.9 0.0 all-gather.6.cloned.1.call-start
  21.9 38.4 %all-reduce.2.cloned.1.call-done = bf16[524288]{0:T(1024)(128)(2,1)} async-done(((bf16[524288]{0:T(1024)(128)(2,1)}), bf16[524288]{0:T(1024)(128)(2,1)}) %all-reduce.2.cloned.1.call-update) | async-done | bytes 1048592 | tf_op jit(solution)/shard_map/psum | solution.py:17
  60.3 5.2 %multiply_convert_fusion.3 = (bf16[524288]{0:T(1024)(128)(2,1)S(1)}, f32[524288]{0:T(1024)}, f32[524288]{0:T(1024)}) fusion(f32[524288]{0:T(1024)} %param.9, bf16[524288]{0:T(1024)(128)(2,1)} %all-reduce.2.cloned.1.call-done, f32[524288]{0:T(1024)} %param.10), kind=kLoop, calls=%fused_computation.7 | loop fusion | flops 5242880 | bytes 10485760 | tf_op jit(solution)/shard_map/convert_element_type | solution.py:26
  65.5 1.4 convert_element_type.57
  67.0 0.0 all-gather.6.cloned.1.call-update
  67.0 0.5 copy-done
  67.5 1.4 copy.18
  68.9 1.4 copy-done.1
  70.3 2.5 %copy.16 = bf16[128,8,1024]{2,0,1:T(8,128)(2,1)} copy(bf16[128,8,1024]{2,1,0:T(8,128)(2,1)S(1)} %bitcast.35) | data formatting | bytes 4194304 | tf_op jit(solution)/shard_map/squeeze | solution.py:20
  72.8 5.8 %all-to-all-start = ((bf16[128,8,1024]{2,0,1:T(8,128)(2,1)}), bf16[128,8,1024]{2,0,1:T(8,128)(2,1)}, u32[]{:S(2)}, u32[]{:S(2)}) async-start(bf16[128,8,1024]{2,0,1:T(8,128)(2,1)} %copy.16), calls=%async_computation | async-start | bytes 4194304 | tf_op jit(solution)/shard_map/all_to_all | solution.py:31
  78.6 0.0 copy-done.5
  78.6 100.9 %all-gather = bf16[1,8192]{1,0:T(2,128)(2,1)S(1)} all-gather(bf16[1,1024]{1,0:T(2,128)(2,1)S(1)} %copy-done.5), channel_id=2, replica_groups=mesh['rep'=4,'fsdp'=8] {'fsdp'}, dimensions={1}, use_global_device_ids=true | all-gather | bytes 18432 | tf_op jit(solution)/shard_map/all_gather | solution.py:43
  179.5 0.1 convert_reduce_fusion
  179.6 0.5 multiply_reduce_fusion
  180.1 20.0 %all-gather.2 = f32[8,1,128]{2,1,0:T(1,128)S(1)} all-gather(f32[1,1,128]{2,1,0:T(1,128)S(1)} %get-tuple-element.8), channel_id=1, replica_groups=mesh['rep'=4,'fsdp'=8] {'fsdp'}, dimensions={0}, use_global_device_ids=true | all-gather | bytes 4608 | tf_op jit(solution)/shard_map/all_gather | solution.py:30
  200.1 0.0 all-to-all-done
  200.1 2.1 multiply_convert_fusion
  202.2 0.0 all-gather.8.cloned.1.call-done
  202.3 4.0 %convolution_bitcast_fusion = f32[1,1024,512]{2,1,0:T(8,128)} fusion(bf16[1024,1024]{1,0:T(8,128)(2,1)S(1)} %multiply_convert_fusion, bf16[1,1024,512]{2,1,0:T(8,128)(2,1)} %all-gather.8.cloned.1.call-done), kind=kOutput, calls=%fused_computation.15 | convolution fusion | flops 1073741824 | bytes 5242880 | tf_op jit(solution)/shard_map/dot_general | solution.py:35
  206.3 3.8 %fusion = f32[1024]{0:T(1024)} fusion(bf16[128,8,1024]{2,0,1:T(8,128)(2,1)} %all-to-all-done, bf16[1024,512]{1,0:T(8,128)(2,1)S(1)} %copy-done.3, f32[1024]{0:T(1024)S(1)} %bitcast.42, bf16[1,1024,512]{2,1,0:T(8,128)(2,1)S(1)} %copy-done.6), kind=kOutput, calls=%fused_computation.2 | convolution fusion | flops 1077935104 | bytes 4202496 | tf_op jit(solution)/shard_map/dot_general | solution.py:38
  210.1 22.3 %all-gather.6.cloned.1.call-done = bf16[8192,512]{1,0:T(8,128)(2,1)} async-done(((bf16[1024,512]{1,0:T(8,128)(2,1)}), bf16[8192,512]{1,0:T(8,128)(2,1)}) %all-gather.6.cloned.1.call-update) | async-done | bytes 8388624 | tf_op jit(solution)/shard_map/all_gather | solution.py:42
  232.4 6.2 %fusion.4 = bf16[8,128,512]{2,1,0:T(8,128)(2,1)S(1)} fusion(bf16[8,1024,512]{2,1,0:T(8,128)(2,1)} %bitcast.43, f32[8,1024]{1,0:T(8,128)S(1)} %reshape.53, f32[128]{0:T(128)S(1)} %get-tuple-element.9, bf16[128,8,1024]{2,1,0:T(8,128)(2,1)S(1)} %bitcast.36), kind=kOutput, calls=%fused_computation.16 | convolution fusion | flops 1078460416 | bytes 11567616 | tf_op jit(solution)/shard_map/tgr,grk->gtk/dot_general | solution.py:47
  238.6 0.8 reduce_sum.31
  (13 shorter events, 0.0 us)
Async XLA Ops:
  8.0 4.7 %copy-start.4 = (f32[1,8192]{1,0:T(1,128)S(1)}, f32[1,8192]{1,0:T(1,128)}, u32[]{:S(2)}) copy-start(f32[1,8192]{1,0:T(1,128)} %param.8) | copy-start | bytes 98308
  8.0 52.3 %all-reduce.2.cloned.1.call-start = ((), (), s32[]{:S(2)}) async-start(), calls=%async_computation.1 | async-start | bytes 2097152 | tf_op jit(solution)/shard_map/psum | solution.py:17
  21.3 181.0 %all-gather.8.cloned.1.call-start = ((), (), s32[]{:S(2)}) async-start(), calls=%async_computation.3 | async-start | bytes 1179648 | tf_op jit(solution)/shard_map/all_gather | solution.py:32
  21.9 210.5 %all-gather.6.cloned.1.call-start = ((), (), s32[]{:S(2)}) async-start(), calls=%async_computation.2 | async-start | bytes 9437184 | tf_op jit(solution)/shard_map/all_gather | solution.py:42
  65.5 2.0 copy-start
  68.9 1.4 copy-start.1
  72.7 5.8 %copy-start.5 = (bf16[1,1024]{1,0:T(2,128)(2,1)S(1)}, bf16[1,1024]{1,0:T(2,128)(2,1)}, u32[]{:S(2)}) copy-start(bf16[1,1024]{1,0:T(2,128)(2,1)} %param.12) | copy-start | bytes 6148
  72.8 127.3 %all-to-all-start = ((bf16[128,8,1024]{2,0,1:T(8,128)(2,1)}), bf16[128,8,1024]{2,0,1:T(8,128)(2,1)}, u32[]{:S(2)}, u32[]{:S(2)}) async-start(bf16[128,8,1024]{2,0,1:T(8,128)(2,1)} %copy.16), calls=%async_computation | async-start | bytes 4194304 | tf_op jit(solution)/shard_map/all_to_all | solution.py:31
  202.2 4.0 %copy-start.3 = (bf16[1024,512]{1,0:T(8,128)(2,1)S(1)}, bf16[1024,512]{1,0:T(8,128)(2,1)}, u32[]{:S(2)}) copy-start(bf16[1024,512]{1,0:T(8,128)(2,1)} %convert_element_type.57) | copy-start | bytes 3145732
  202.3 4.0 %copy-start.6 = (bf16[1,1024,512]{2,1,0:T(8,128)(2,1)S(1)}, bf16[1,1024,512]{2,1,0:T(8,128)(2,1)}, u32[]{:S(2)}) copy-start(bf16[1,1024,512]{2,1,0:T(8,128)(2,1)} %all-gather.8.cloned.1.call-done) | copy-start | bytes 3145732
  206.3 26.1 %copy-start.2 = (bf16[16,8,8,1024]{3,2,1,0:T(8,128)(2,1)S(1)}, bf16[16,8,8,1024]{3,2,1,0:T(8,128)(2,1)}, u32[]{:S(2)}) copy-start(bf16[16,8,8,1024]{3,2,1,0:T(8,128)(2,1)} %copy-done.1) | copy-start | bytes 6291460
Sparse Core Ops, SparseCore 0:
  21.4 38.8 all-reduce.1
Sparse Core Ops, SparseCore 1:
  24.1 43.1 all-gather.7
  69.5 162.8 all-gather.5
where the time goes:
time: 247 us
  blocking collectives  121 us (49%)
  waiting for transfers between devices  61.2 us (25%)
  other arithmetic  16.2 us (7%)
  between operations  15.6 us (6%)
  matrix products  14 us (6%)
  local copies, waits for them, and re-layouts  13 us (5%)
  starting transfers between devices  5.94 us (2%)
    all_gather x1, blocking collectives, shards(): gain_piece = lax.all_gather(own_gain, 'fsdp', axis=0, tiled=True)  101 us
    psum x1, waiting for transfers between devices, shards(): lax.psum(decoded.astype(jnp.bfloat16), 'rep').astype(jnp.float32) / replicas  38.4 us
    all_gather x1, waiting for transfers between devices, shards(): weight_piece = lax.all_gather(own_weight, 'fsdp', axis=0, tiled=True)  22.3 us
    all_gather x1, blocking collectives, shards(): every_scale = lax.all_gather(inv_rms, 'fsdp', axis=0, tiled=True)  20 us
    dot_general x1, matrix products, shards(): jnp.einsum('tgr,grk->gtk', normed.reshape(tok_rows, blocks, own_rows), we...  6.23 us
    all_to_all x1, starting transfers between devices, shards(): lax.all_to_all(activations, 'fsdp', split_axis=1, concat_axis=0, tiled=True)  5.82 us
    convert_element_type x1, other arithmetic, shards(): (new_base.reshape(own_rows, key_width) * D ** (-0.5)).astype(jnp.bfloat16)  5.22 us
  transfers between devices with their start and end apart: 4, of which 2 were waited for; matrix products, arithmetic and copies ran while one was open for 9% of the time, Pallas kernels for 0%

commit v1 on v0

v1 whole, which is shorter than its diff:
```python
import functools

import jax
import jax.numpy as jnp
from jax import lax
from jax.experimental import pallas as pl
from jax.experimental.pallas import tpu as pltpu
from jax.sharding import PartitionSpec as P

D = 8192
BLOCK = 64
LANES = 128
RIDER = 2
VMEM_LIMIT = 32 * 1024 * 1024


outer_rate = 0.7
momentum_decay = 0.9


def swap(value, axis, bit):
    return lax.ppermute(value, axis, [(i, i ^ bit) for i in range(lax.axis_size(axis))])


def params():
    return pltpu.CompilerParams(vmem_limit_bytes=VMEM_LIMIT)


def pack(block, width):
    tokens, key_width = block.shape
    if width >= key_width:
        rows = tokens * key_width // width
        return jnp.concatenate([block[at : at + rows] for at in range(0, tokens, rows)], axis=1)
    return jnp.concatenate([block[:, c : c + width] for c in range(0, key_width, width)], axis=0)


def unpack(rows, tokens, key_width):
    width = rows.shape[1]
    if width >= key_width:
        return jnp.concatenate([rows[:, c : c + key_width] for c in range(0, width, key_width)], axis=0)
    return jnp.concatenate([rows[at : at + tokens] for at in range(0, rows.shape[0], tokens)], axis=1)


def scale_kernel(me_ref, x_ref, near_ref, *far_refs):
    rows, features = x_ref.shape
    near, _, width = near_ref.shape
    step = 16
    first = me_ref[0] & ~(near - 1)

    @pl.loop(0, rows // step)
    def _(i):
        here = pl.ds(pl.multiple_of(i * step, step), step)
        total = jnp.zeros((step, LANES), jnp.float32)
        for c in range(0, features, LANES):
            part = x_ref[here, c : c + LANES].astype(jnp.float32)
            total = total + part * part
        mean = jnp.sum(total, axis=1, keepdims=True) * (1.0 / features)
        inv_rms = lax.rsqrt(mean + 1e-05)
        for at in range(near + len(far_refs)):
            owner = first + at if at < near else me_ref[0] ^ at
            start = pl.multiple_of(owner * width, width)
            part = x_ref[here, pl.ds(start, width)].astype(jnp.float32)
            part = (part * inv_rms).astype(jnp.bfloat16)
            if at < near:
                near_ref[at, here, :] = part
            else:
                far_refs[at - near][here, :] = part


def scale_inputs(activations, me, owners, above):
    tokens, features = activations.shape
    width = features // owners
    far = owners // 2
    rows = 32
    skips = [above if at == RIDER else 0 for at in range(far)]
    return pl.pallas_call(
        scale_kernel,
        grid_spec=pltpu.PrefetchScalarGridSpec(
            num_scalar_prefetch=1,
            grid=(tokens // rows,),
            in_specs=[pl.BlockSpec((rows, features), lambda i, me: (i, 0))],
            out_specs=[pl.BlockSpec((far, rows, width), lambda i, me: (0, i, 0))]
            + [pl.BlockSpec((rows, width), lambda i, me, skip=skip: (i + skip // rows, 0)) for skip in skips],
        ),
        out_shape=[jax.ShapeDtypeStruct((far, tokens, width), jnp.bfloat16)]
        + [jax.ShapeDtypeStruct((tokens + skip, width), jnp.bfloat16) for skip in skips],
        compiler_params=params(),
        cost_estimate=pl.CostEstimate(
            flops=4 * tokens * features, bytes_accessed=4 * tokens * features, transcendentals=tokens
        ),
        name="scale_inputs",
    )(me, activations)


def decode_kernel(half_ref, codes_ref, scales_ref, out_ref):
    group_rows = BLOCK
    row = lax.broadcasted_iota(jnp.int32, (group_rows, LANES), 0)
    lane = lax.broadcasted_iota(jnp.int32, (group_rows, LANES), 1)
    per_row = LANES // BLOCK
    own = lane // per_row == row
    k = lax.broadcasted_iota(jnp.int32, (2 * LANES, LANES), 0)
    n = lax.broadcasted_iota(jnp.int32, (2 * LANES, LANES), 1)
    spread = (k % per_row == n // BLOCK).astype(jnp.float32).astype(jnp.bfloat16)
    pieces = []
    for group in range(scales_ref.shape[0]):
        wide = jnp.broadcast_to(scales_ref[group : group + 1, :], (group_rows, LANES))
        wide = jnp.where(own, wide, 0.0)
        high = wide.astype(jnp.bfloat16)
        low = (wide - high.astype(jnp.float32)).astype(jnp.bfloat16)
        pieces.append(jnp.concatenate([high, low], axis=1))
    scale = jnp.dot(jnp.concatenate(pieces, axis=0), spread, preferred_element_type=jnp.float32)
    out_ref[...] = ((codes_ref[...] - 8).astype(jnp.float32) * scale).astype(jnp.bfloat16)


def decode(codes, scales, half):
    rows = codes.shape[0] // 2
    groups = scales.shape[0] // 2
    step = min(8, groups)
    steps = groups // step
    return pl.pallas_call(
        decode_kernel,
        grid_spec=pltpu.PrefetchScalarGridSpec(
            num_scalar_prefetch=1,
            grid=(steps,),
            in_specs=[
                pl.BlockSpec((rows // steps, LANES), lambda i, half: (half[0] * steps + i, 0)),
                pl.BlockSpec((step, LANES), lambda i, half: (half[0] * steps + i, 0)),
            ],
            out_specs=pl.BlockSpec((rows // steps, LANES), lambda i, half: (i, 0)),
        ),
        out_shape=jax.ShapeDtypeStruct((rows, LANES), jnp.bfloat16),
        compiler_params=params(),
        cost_estimate=pl.CostEstimate(flops=2 * rows * LANES, bytes_accessed=6 * rows * LANES, transcendentals=0),
        name="decode",
    )(half, codes, scales)


def update_kernel(replicas, core_ref, mine_ref, other_ref, base_ref, momentum_ref, base_out, momentum_out, weight_ref):
    own = pl.program_id(0) == core_ref[0]
    total = jnp.where(own, mine_ref[...].astype(jnp.float32), other_ref[...].astype(jnp.float32))
    average = total * (1.0 / replicas)
    new_momentum = momentum_decay * momentum_ref[...] + average
    momentum_out[...] = new_momentum
    base_out[...] = base_ref[...] - outer_rate * (average + momentum_decay * new_momentum)
    rows, width = weight_ref.shape
    cuts = width // LANES
    for c in range(cuts):
        part = base_out[pl.ds(c, rows, cuts), :]
        weight_ref[:, c * LANES : (c + 1) * LANES] = (part * D ** (-0.5)).astype(jnp.bfloat16)


def update(mine, other, core, base, momentum, replicas, key_width):
    rows = mine.shape[0]
    steps = 2
    weight_rows = 2 * rows * LANES // key_width
    half = pl.BlockSpec((rows // steps, LANES), lambda h, i, core: (i, 0))
    whole = pl.BlockSpec((rows // steps, LANES), lambda h, i, core: (h * steps + i, 0))
    full = jax.ShapeDtypeStruct((2 * rows, LANES), jnp.float32)
    return pl.pallas_call(
        functools.partial(update_kernel, replicas),
        grid_spec=pltpu.PrefetchScalarGridSpec(
            num_scalar_prefetch=1,
            grid=(2, steps),
            in_specs=[half, half, whole, whole],
            out_specs=[
                whole,
                whole,
                pl.BlockSpec((weight_rows // 2 // steps, key_width), lambda h, i, core: (h * steps + i, 0)),
            ],
        ),
        out_shape=[full, full, jax.ShapeDtypeStruct((weight_rows, key_width), jnp.bfloat16)],
        compiler_params=params(),
        cost_estimate=pl.CostEstimate(flops=12 * rows * LANES, bytes_accessed=40 * rows * LANES, transcendentals=0),
        name="update",
    )(core, mine, other, base, momentum)


def store_cuts(out_refs, orders, slot, part):
    cut = part.shape[1] // len(out_refs)
    for at, (out_ref, order) in enumerate(zip(out_refs, orders)):
        out_ref[order.index(slot)] = part[:, at * cut : (at + 1) * cut]


def near_keys_kernel(orders, me_ref, x_ref, weight_ref, gain_ref, *out_refs):
    gain = gain_ref[...].astype(jnp.float32)
    weight = weight_ref[...]
    near, tokens, _ = out_refs[0].shape
    for slot in range(near):
        x = x_ref[(me_ref[0] & (near - 1)) ^ slot, x_ref.shape[1] - tokens :, :]
        normed = (x.astype(jnp.float32) * gain).astype(jnp.bfloat16)
        part = jnp.dot(normed, weight, preferred_element_type=jnp.float32).astype(jnp.bfloat16)
        store_cuts(out_refs, orders, slot, part)


def near_partial_keys(columns, me, tokens, orders, weight, gain):
    near, _, width = columns.shape
    key_width = weight.shape[1]
    flops = 2 * near * tokens * width * key_width
    whole = pl.BlockSpec(memory_space=pltpu.VMEM)
    cut = jax.ShapeDtypeStruct((near, tokens, key_width // len(orders)), jnp.bfloat16)
    return pl.pallas_call(
        functools.partial(near_keys_kernel, orders),
        in_specs=[pl.BlockSpec(memory_space=pltpu.SMEM), whole, whole, whole],
        out_specs=[whole] * len(orders),
        out_shape=[cut] * len(orders),
        compiler_params=params(),
        cost_estimate=pl.CostEstimate(flops=flops, bytes_accessed=flops // 256, transcendentals=0),
        name="near_partial_keys",
    )(me, columns, weight, gain)


def far_keys_kernel(orders, *refs):
    *x_refs, weight_ref, gain_ref = refs[: -len(orders)]
    out_refs = refs[-len(orders) :]
    gain = gain_ref[...].astype(jnp.float32)
    weight = weight_ref[...]
    tokens = out_refs[0].shape[1]
    for slot, x_ref in enumerate(x_refs):
        x = x_ref[x_ref.shape[0] - tokens :, :]
        normed = (x.astype(jnp.float32) * gain).astype(jnp.bfloat16)
        part = jnp.dot(normed, weight, preferred_element_type=jnp.float32).astype(jnp.bfloat16)
        store_cuts(out_refs, orders, slot, part)


def far_partial_keys(blocks, tokens, orders, weight, gain):
    width, key_width = weight.shape
    flops = 2 * len(blocks) * tokens * width * key_width
    cut = jax.ShapeDtypeStruct((len(blocks), tokens, key_width // len(orders)), jnp.bfloat16)
    return pl.pallas_call(
        functools.partial(far_keys_kernel, orders),
        out_shape=[cut] * len(orders),
        compiler_params=params(),
        cost_estimate=pl.CostEstimate(flops=flops, bytes_accessed=flops // 256, transcendentals=0),
        name="far_partial_keys",
    )(*blocks, weight, gain)


def by_bits(count, bits):
    return sorted(range(count), key=lambda slot: [bool(slot & bit) for bit in bits])


def fold(near, far, bits, spread):
    for bit in bits:
        middle = near.shape[0] // 2
        got = swap(jnp.concatenate([near[middle:], far[middle:], spread], axis=0), "fsdp", bit)
        near = add(near[:middle], got[:middle])
        far = add(far[:middle], got[middle : 2 * middle])
        spread = jnp.concatenate([spread, got[2 * middle :]], axis=0)
    return near[0], far[0], spread


def spread_slots(bits):
    slots = [0]
    for bit in bits:
        slots = slots + [slot ^ bit for slot in slots]
    return slots


def add(*parts):
    return sum(part.astype(jnp.float32) for part in parts).astype(jnp.bfloat16)


def grads_kernel(orders, me_ref, x_ref, gain_ref, weight_ref, *refs):
    *others, rows_ref, total_ref = refs
    far_refs, token_refs = others[: -len(orders)], others[-len(orders) :]
    near, rows, _ = x_ref.shape
    tokens, key_width = token_refs[0].shape[1], weight_ref.shape[1]
    i = pl.program_id(0)
    cut = rows_ref.shape[0]
    columns = pl.ds(pl.multiple_of(i * cut, cut), cut)
    blocks, upstream = [], []
    for slot in range(near):
        at = (me_ref[0] & (near - 1)) ^ slot
        far_ref = far_refs[slot ^ RIDER]
        blocks += [x_ref[at, rows - tokens :, columns], far_ref[far_ref.shape[0] - tokens :, :]]
        upstream += [
            unpack(x_ref[at, : rows - tokens, :], tokens, key_width),
            jnp.concatenate([ref[order.index(slot)] for ref, order in zip(token_refs, orders)], axis=1),
        ]
    x = jnp.concatenate(blocks, axis=0).astype(jnp.float32)
    upstream = jnp.concatenate(upstream, axis=0)
    normed = (x * gain_ref[...].astype(jnp.float32)).astype(jnp.bfloat16)
    rows_ref[...] = lax.dot_general(
        normed, upstream, (((0,), (0,)), ((), ())), preferred_element_type=jnp.float32
    )
    back = lax.dot_general(
        upstream, weight_ref[...], (((1,), (1,)), ((), ())), preferred_element_type=jnp.float32
    )
    total_ref[...] = jnp.sum(back * x, axis=0, keepdims=True)


def grads(columns, far_blocks, far_tokens, orders, me, gain, weight):
    near, _, width = columns.shape
    tokens, key_width = far_tokens[0].shape[1], weight.shape[1]
    cut = min(256, width)
    flops = 8 * near * tokens * width * key_width
    return pl.pallas_call(
        functools.partial(grads_kernel, orders),
        grid_spec=pltpu.PrefetchScalarGridSpec(
            num_scalar_prefetch=1,
            grid=(width // cut,),
            in_specs=[
                pl.BlockSpec(columns.shape, lambda i, me: (0, 0, 0)),
                pl.BlockSpec((1, cut), lambda i, me: (0, i)),
                pl.BlockSpec((cut, key_width), lambda i, me: (i, 0)),
            ]
            + [pl.BlockSpec((block.shape[0], cut), lambda i, me: (0, i)) for block in far_blocks]
            + [pl.BlockSpec(one.shape, lambda i, me: (0, 0, 0)) for one in far_tokens],
            out_specs=[
                pl.BlockSpec((cut, key_width), lambda i, me: (i, 0)),
                pl.BlockSpec((1, cut), lambda i, me: (0, i)),
            ],
        ),
        out_shape=[
            jax.ShapeDtypeStruct((width, key_width), jnp.float32),
            jax.ShapeDtypeStruct((1, width), jnp.float32),
        ],
        compiler_params=params(),
        cost_estimate=pl.CostEstimate(flops=flops, bytes_accessed=flops // 512, transcendentals=0),
        name="grads",
    )(me, columns, gain, weight, *far_blocks, *far_tokens)


def sum_over_replicas(codes, scales, core):
    give = decode(codes, scales, 1 - core)
    keep = decode(codes, scales, core)
    total = keep.astype(jnp.float32) + swap(give, "rep", 1).astype(jnp.float32)
    bit = 2
    while bit < lax.axis_size("rep"):
        mine = total.astype(jnp.bfloat16)
        total = mine.astype(jnp.float32) + swap(mine, "rep", bit).astype(jnp.float32)
        bit *= 2
    mine = total.astype(jnp.bfloat16)
    return mine, swap(mine, "rep", 1)


def stage(work, *operands):
    def nothing(*operands):
        made = jax.eval_shape(work, *operands)
        return tuple(jnp.zeros(one.shape, one.dtype) for one in made)

    return lax.cond(lax.axis_index("fsdp") < lax.axis_size("fsdp"), work, nothing, *operands)


def shards(codes, scales, base, momentum, inputs, gain, cotangent):
    activations = inputs[0]
    upstream = cotangent[0]
    tokens, key_width = upstream.shape
    owners = lax.axis_size("fsdp")
    replicas = lax.axis_size("rep")
    me = lax.axis_index("fsdp").astype(jnp.int32)[None]
    core = (lax.axis_index("rep").astype(jnp.int32) & 1)[None]
    far = owners // 2
    bits = [1 << k for k in range(far.bit_length() - 1)]

    width = activations.shape[1] // owners
    packed = pack(upstream, width)
    above = packed.shape[0]
    near, *scaled = scale_inputs(activations, me, owners, above)
    near, *scaled, codes = lax.optimization_barrier((near, *scaled, codes))
    scaled[RIDER] = scaled[RIDER].at[:above].set(packed)
    far_blocks = [swap(scaled[slot], "fsdp", far + slot) for slot in range(far)]

    halves = [[half * far + i for i in range(far)] for half in range(2)]
    swapped = [bits[1], bits[0]] + bits[2:]
    orders = [by_bits(far, each) for each in (bits, swapped)]

    def beside(codes, scales, base, momentum, near, packed, gain):
        near = jnp.concatenate([jnp.broadcast_to(packed, (far, *packed.shape)), near], axis=1)
        columns = lax.all_to_all(near, "fsdp", split_axis=0, concat_axis=0, tiled=True, axis_index_groups=halves)
        mine, other = sum_over_replicas(codes, scales, core)
        updated = update(mine, other, core, base, momentum, replicas, key_width)
        weight = updated[-1]
        return *updated, columns, *near_partial_keys(columns, me, tokens, orders, weight, gain)

    new_base, new_momentum, weight, columns, *near_parts = stage(
        beside,
        codes.reshape(-1, LANES),
        scales.reshape(-1, LANES),
        base.reshape(-1, LANES),
        momentum.reshape(-1, LANES),
        near,
        packed,
        gain,
    )

    rider = far_blocks[RIDER]
    far_tokens = jnp.split(unpack(rider[: rider.shape[0] - tokens], tokens, key_width)[None], 2, axis=2)
    far_parts = far_partial_keys(far_blocks, tokens, orders, weight, gain)
    folded = [fold(*each) for each in zip(near_parts, far_parts, (bits, swapped), far_tokens)]
    own, given, spread = zip(*folded)
    given, columns, *spread = lax.optimization_barrier((jnp.concatenate(given, axis=1), columns, *spread))
    keys = add(jnp.concatenate(own, axis=1), swap(given, "fsdp", far))

    slots = [spread_slots(bits), spread_slots(swapped)]
    grad_rows, grad_total = grads(columns, far_blocks, spread, slots, me, gain, weight)
    return (
        new_base.reshape(-1),
        new_momentum.reshape(-1),
        keys[None],
        grad_rows[None],
        grad_total,
    )


def solution(mesh):
    placed = (
        P("rep", "fsdp"),
        P("rep", "fsdp"),
        P("fsdp"),
        P("fsdp"),
        P("rep", "fsdp", None),
        P("rep", "fsdp"),
        P("rep", "fsdp", None),
    )
    return jax.shard_map(
        shards,
        mesh=mesh,
        in_specs=placed,
        out_specs=(
            P("fsdp"),
            P("fsdp"),
            P("rep", "fsdp", None),
            P("rep", "fsdp", None),
            P("rep", "fsdp"),
        ),
        check_vma=False,
    )
```

time: 247 us -> 91.1 us (0.37)
  blocking collectives: 121 us -> 0 us
  Pallas kernels: 0 us -> 21 us
  waiting for transfers between devices: 61.2 us -> 44.8 us
  between operations: 15.6 us -> 0.92 us
  matrix products: 14 us -> 0 us
  other arithmetic: 16.2 us -> 2.7 us
  starting transfers between devices: 5.94 us -> 19.3 us
  local copies, waits for them, and re-layouts: 13 us -> 1.79 us
    all_gather x2 -> x0, blocking collectives: 121 us -> none  [the longest x1 101 us: shards(): gain_piece = lax.all_gather(own_gain, 'fsdp', axis=0, tiled=True)]
    psum x1 -> x0, waiting for transfers between devices: 38.4 us -> none  [shards(): lax.psum(decoded.astype(jnp.bfloat16), 'rep').astype(jnp.float32) / replicas]
    ppermute x0 -> x12, waiting for transfers between devices: none -> 30.2 us  [swap(): lax.ppermute(value, axis, [(i, i ^ bit) for i in range(lax.axis_size(axis...]
    all_gather x2 -> x0, waiting for transfers between devices: 22.3 us -> none  [the longest x1 22.3 us: shards(): weight_piece = lax.all_gather(own_weight, 'fsdp', axis=0, tiled=True)]
    pallas_call x0 -> x7, Pallas kernels: none -> 21 us  [the longest x2 5.59 us: decode(): pl.pallas_call(decode_kernel, grid_spec=pltpu.PrefetchScalarGridSpec(num_...]
    ppermute x0 -> x12, starting transfers between devices: none -> 14.8 us  [swap(): lax.ppermute(value, axis, [(i, i ^ bit) for i in range(lax.axis_size(axis...]
    all_to_all x1, waiting for transfers between devices: 0.01 us -> 14.6 us  [beside(): lax.all_to_all(near, 'fsdp', split_axis=0, concat_axis=0, tiled=True, axi...]
    convert_element_type x4, other arithmetic: 14.8 us -> 0.42 us  [the longest x2 0.28 us: sum_over_replicas(): mine = total.astype(jnp.bfloat16)]
  transfers between devices with their start and end apart: 4 -> 13, of which waited for: 2 -> 7; matrix products, arithmetic and copies ran while one was open for 9% -> 2% of each run, Pallas kernels for 0% -> 18%
where the time goes in v1:
time: 91.1 us; the launch traced here: 90.5 us
  waiting for transfers between devices  44.8 us (49%)
  Pallas kernels  21 us (23%)
  starting transfers between devices  19.3 us (21%)
  other arithmetic  2.7 us (3%)
  local copies, waits for them, and re-layouts  1.79 us (2%)
  between operations  0.92 us (1%)
    ppermute x12, waiting for transfers between devices, swap(): lax.ppermute(value, axis, [(i, i ^ bit) for i in range(lax.axis_size(axis...  30.2 us
    ppermute x12, starting transfers between devices, swap(): lax.ppermute(value, axis, [(i, i ^ bit) for i in range(lax.axis_size(axis...  14.8 us
    all_to_all x1, waiting for transfers between devices, beside(): lax.all_to_all(near, 'fsdp', split_axis=0, concat_axis=0, tiled=True, axi...  14.6 us
    pallas_call x2, Pallas kernels, decode(): pl.pallas_call(decode_kernel, grid_spec=pltpu.PrefetchScalarGridSpec(num_...  5.59 us
    pallas_call x1, Pallas kernels, grads(): pl.pallas_call(functools.partial(grads_kernel, orders), grid_spec=pltpu.P...  5.45 us
    all_to_all x1, starting transfers between devices, beside(): lax.all_to_all(near, 'fsdp', split_axis=0, concat_axis=0, tiled=True, axi...  4.48 us
    pallas_call x1, Pallas kernels, update(): pl.pallas_call(functools.partial(update_kernel, replicas), grid_spec=pltp...  2.95 us
    pallas_call x1, Pallas kernels, scale_inputs(): pl.pallas_call(scale_kernel, grid_spec=pltpu.PrefetchScalarGridSpec(num_s...  2.61 us
  transfers between devices with their start and end apart: 13, of which 7 were waited for; matrix products, arithmetic and copies ran while one was open for 2% of the time, Pallas kernels for 18%

profile of v1, /device:TPU:0, one launch (start us, length us, event | category | flops | bytes accessed | tf_op | source)
XLA Modules:
  0.0 90.5 jit_solution(17812615608704219942)
XLA Ops:
  0.7 1.6 %copy-done = bf16[1,128,8192]{2,1,0:T(8,128)(2,1)S(1)} copy-done((bf16[1,128,8192]{2,1,0:T(8,128)(2,1)S(1)}, bf16[1,128,8192]{2,1,0:T(8,128)(2,1)}, u32[]{:S(2)}) %copy-start) | copy-done | bytes 2097176
  2.2 2.6 %scale_inputs.1 = (bf16[4,128,1024]{2,1,0:T(8,128)(2,1)}, bf16[128,1024]{1,0:T(8,128)(2,1)S(1)}, bf16[128,1024]{1,0:T(8,128)(2,1)S(1)}, bf16[192,1024]{1,0:T(8,128)(2,1)S(1)}, bf16[128,1024]{1,0:T(8,128)(2,1)S(1)}) custom-call(s32[1]{0:T(128)} %bitcast.7.me_ref, bf16[128,8192]{1,0:T(8,128)(2,1)S(1)} %bitcast.26), custom_call_target="tpu_custom_call" | custom-call | flops 4194304 | bytes 4194304 | tf_op jit(solution)/shard_map/scale_inputs/pallas_call | solution.py:76
  4.9 5.1 %collective-permute-start.5 = (bf16[192,1024]{1,0:T(8,128)(2,1)S(1)}, bf16[192,1024]{1,0:T(8,128)(2,1)S(1)}, u32[]{:S(2)}, u32[]{:S(2)}) collective-permute-start(bf16[192,1024]{1,0:T(8,128)(2,1)S(1)} %get-tuple-element.126), channel_id=1, source_target_pairs={{0,6},{1,7},{2,4},{3,5},{4,2},{5,3},{6,0},{7,1},{8,14},{9,15},{10,... | collective-permute-start | bytes 1179656 | tf_op jit(solution)/shard_map/ppermute | solution.py:22
  10.0 3.8 %collective-permute-start.4 = (bf16[128,1024]{1,0:T(8,128)(2,1)S(1)}, bf16[128,1024]{1,0:T(8,128)(2,1)S(1)}, u32[]{:S(2)}, u32[]{:S(2)}) collective-permute-start(bf16[128,1024]{1,0:T(8,128)(2,1)S(1)} %get-tuple-element.94), channel_id=1, source_target_pairs={{0,5},{1,4},{2,7},{3,6},{4,1},{5,0},{6,3},{7,2},{8,13},{9,12},{10,... | collective-permute-start | bytes 786440 | tf_op jit(solution)/shard_map/ppermute | solution.py:22
  13.9 48.2 %conditional.1 = (bf16[1024,512]{1,0:T(8,128)(2,1)}, bf16[4,192,1024]{2,1,0:T(8,128)(2,1)}, bf16[4,128,256]{2,1,0:T(8,128)(2,1)S(1)}, bf16[4,128,256]{2,1,0:T(8,...) conditional(s32[]{:T(128)} %convert_element_type.102, () %tuple.27, (s32[]{:T(128)}, s32[1,524288]{1,0:T(1,128)}, ...), branch_computations={%region_0.0_spmd, %region_1.0_spmd} | conditional | flops 546308096 | bytes 54788432 | solution.py:342
  13.9 2.8 %decode.3 = bf16[2048,128]{1,0:T(8,128)(2,1)S(1)} custom-call(s32[1]{0:T(128)S(6)} %sub.2.half_ref, s32[4096,128]{1,0:T(8,128)} %bitcast.27, f32[64,128]{1,0:T(8,128)} %bitcast.31), custom_call_target="tpu_custom_call" | custom-call | flops 524288 | bytes 1572864 | tf_op jit(solution)/shard_map/cond/branch_1_fun/decode/pallas_call | solution.py:120
  16.7 0.1 collective-permute-start
  16.8 1.3 %pad_maximum_fusion = bf16[4,192,1024]{2,1,0:T(8,128)(2,1)} fusion(bf16[4,128,1024]{2,1,0:T(8,128)(2,1)S(1)} %copy-done.3, bf16[4,64,1024]{2,1,0:T(8,128)(2,1)S(1)} %broadcast_in_dim.14), kind=kLoop, calls=%fused_computation | loop fusion | flops 3145728 | bytes 3145728 | tf_op jit(solution)/shard_map/cond/branch_1_fun/concatenate | solution.py:369
  18.1 4.5 %all-to-all-start = ((bf16[4,192,1024]{2,1,0:T(8,128)(2,1)}), bf16[4,192,1024]{2,1,0:T(8,128)(2,1)}, u32[]{:S(2)}, u32[]{:S(2)}) async-start(bf16[4,192,1024]{2,1,0:T(8,128)(2,1)} %pad_maximum_fusion), calls=%async_computation | async-start | bytes 3145728 | tf_op jit(solution)/shard_map/cond/branch_1_fun/all_to_all | solution.py:370
  22.6 2.8 %decode.2 = bf16[2048,128]{1,0:T(8,128)(2,1)S(1)} custom-call(s32[1]{0:T(128)} %bitcast.half_ref.core_ref, s32[4096,128]{1,0:T(8,128)} %bitcast.28, f32[64,128]{1,0:T(8,128)S(1)} %bitcast.32), custom_call_target="tpu_custom_call" | custom-call | flops 524288 | bytes 1572864 | tf_op jit(solution)/shard_map/cond/branch_1_fun/decode/pallas_call | solution.py:120
  25.5 0.1 add_convert_fusion.1
  25.6 1.7 %collective-permute-start.1 = (bf16[2048,128]{1,0:T(8,128)(2,1)S(1)}, bf16[2048,128]{1,0:T(8,128)(2,1)S(1)}, u32[]{:S(2)}, u32[]{:S(2)}) collective-permute-start(bf16[2048,128]{1,0:T(8,128)(2,1)S(1)} %add_convert_fusion.1), channel_id=1, source_target_pairs={{0,16},{8,24},{16,0},{24,8},{1,17},{9,25},{17,1},{25,9},{2,18},{10... | collective-permute-start | bytes 1572872 | tf_op jit(solution)/shard_map/cond/branch_1_fun/ppermute | solution.py:22
  27.4 12.7 %collective-permute-done.1 = bf16[2048,128]{1,0:T(8,128)(2,1)S(1)} collective-permute-done((bf16[2048,128]{1,0:T(8,128)(2,1)S(1)}, bf16[2048,128]{1,0:T(8,128)(2,1)S(1)}, u32[]{:S(2)}, u32[]{:S(2)}) %collective-permute-start.1) | collective-permute-done | bytes 524320 | tf_op jit(solution)/shard_map/cond/branch_1_fun/ppermute | solution.py:22
  40.0 0.1 add_convert_fusion.mine_ref
  40.2 0.1 collective-permute-start.2
  40.2 1.9 %collective-permute-done.2.other_ref = bf16[2048,128]{1,0:T(8,128)(2,1)S(1)} collective-permute-done((bf16[2048,128]{1,0:T(8,128)(2,1)S(1)}, bf16[2048,128]{1,0:T(8,128)(2,1)S(1)}, u32[]{:S(2)}, u32[]{:S(2)}) %collective-permute-start.2) | collective-permute-done | bytes 524320 | tf_op jit(solution)/shard_map/cond/branch_1_fun/ppermute | solution.py:22
  42.1 2.9 %update.1 = (f32[4096,128]{1,0:T(8,128)}, f32[4096,128]{1,0:T(8,128)}, bf16[1024,512]{1,0:T(8,128)(2,1)}) custom-call(s32[1]{0:T(128)} %bitcast.half_ref.core_ref, bf16[2048,128]{1,0:T(8,128)(2,1)S(1)} %add_convert_fusion.mine_ref, bf16[2048,128]{1,0:T(8,128)(2,1)S(1)} %collective-permute-done.2.other_ref, f32[4096,128]{1,0:T(8,128)S(1)} %bitcast.29, ...), custom_call_target="tpu_custom_call" | custom-call | flops 3145728 | bytes 10485760 | tf_op jit(solution)/shard_map/cond/branch_1_fun/update/pallas_call | solution.py:159
  45.1 14.6 %all-to-all-done.x_ref = bf16[4,192,1024]{2,1,0:T(8,128)(2,1)} async-done(((bf16[4,192,1024]{2,1,0:T(8,128)(2,1)}), bf16[4,192,1024]{2,1,0:T(8,128)(2,1)}, u32[]{:S(2)}, u32[]{:S(2)}) %all-to-all-start) | async-done | bytes 1572896 | tf_op jit(solution)/shard_map/cond/branch_1_fun/all_to_all | solution.py:370
  59.7 2.4 %near_partial_keys.1 = (bf16[4,128,256]{2,1,0:T(8,128)(2,1)S(1)}, bf16[4,128,256]{2,1,0:T(8,128)(2,1)S(1)}) custom-call(s32[1]{0:T(128)} %get-tuple-element.47.me_ref, bf16[4,192,1024]{2,1,0:T(8,128)(2,1)} %all-to-all-done.x_ref, bf16[1024,512]{1,0:T(8,128)(2,1)} %get-tuple-element.136.weight_ref, bf16[1,1024]{1,0:T(2,128)(2,1)S(1)} %get-tuple-element.48.gain_ref), custom_call_target="tpu_custom_call" | custom-call | flops 536870912 | bytes 2097152 | tf_op jit(solution)/shard_map/cond/branch_1_fun/near_partial_keys/pallas_call | solution.py:201
  62.2 1.9 %far_partial_keys.1 = (bf16[4,128,256]{2,1,0:T(8,128)(2,1)S(1)}, bf16[4,128,256]{2,1,0:T(8,128)(2,1)S(1)}) custom-call(bf16[128,1024]{1,0:T(8,128)(2,1)S(1)} %collective-permute-done.3.refs_0_, bf16[128,1024]{1,0:T(8,128)(2,1)S(1)} %collective-permute-done.4.refs_1_, bf16[192,1024]{1,0:T(8,128)(2,1)S(1)} %collective-permute-done.5.refs_2_, ...), custom_call_target="tpu_custom_call" | custom-call | flops 536870912 | bytes 2097152 | tf_op jit(solution)/shard_map/far_partial_keys/pallas_call | solution.py:229
  64.3 0.1 collective-permute-start.9
  64.4 1.5 %collective-permute-start.7 = (bf16[5,128,256]{2,1,0:T(8,128)(2,1)S(1)}, bf16[5,128,256]{2,1,0:T(8,128)(2,1)S(1)}, u32[]{:S(2)}, u32[]{:S(2)}) collective-permute-start(bf16[5,128,256]{2,1,0:T(8,128)(2,1)S(1)} %pad_maximum_fusion.1), channel_id=1, source_target_pairs={{0,1},{1,0},{2,3},{3,2},{4,5},{5,4},{6,7},{7,6},{8,9},{9,8},{10,11... | collective-permute-start | bytes 983048 | tf_op jit(solution)/shard_map/ppermute | solution.py:22
  66.0 7.7 %collective-permute-done.9 = bf16[5,128,256]{2,1,0:T(8,128)(2,1)S(1)} collective-permute-done((bf16[5,128,256]{2,1,0:T(8,128)(2,1)S(1)}, bf16[5,128,256]{2,1,0:T(8,128)(2,1)S(1)}, u32[]{:S(2)}, u32[]{:S(2)}) %collective-permute-start.9) | collective-permute-done | bytes 327712 | tf_op jit(solution)/shard_map/ppermute | solution.py:22
  73.7 0.1 add_convert_fusion.4
  73.8 1.5 %collective-permute-start.10 = (bf16[4,128,256]{2,1,0:T(8,128)(2,1)S(1)}, bf16[4,128,256]{2,1,0:T(8,128)(2,1)S(1)}, u32[]{:S(2)}, u32[]{:S(2)}) collective-permute-start(bf16[4,128,256]{2,1,0:T(8,128)(2,1)S(1)} %pad_maximum_fusion.4), channel_id=1, source_target_pairs={{0,1},{1,0},{2,3},{3,2},{4,5},{5,4},{6,7},{7,6},{8,9},{9,8},{10,11... | collective-permute-start | bytes 786440 | tf_op jit(solution)/shard_map/ppermute | solution.py:22
  75.5 0.4 collective-permute-start.8
  75.9 5.1 %collective-permute-done.10 = bf16[4,128,256]{2,1,0:T(8,128)(2,1)S(1)} collective-permute-done((bf16[4,128,256]{2,1,0:T(8,128)(2,1)S(1)}, bf16[4,128,256]{2,1,0:T(8,128)(2,1)S(1)}, u32[]{:S(2)}, u32[]{:S(2)}) %collective-permute-start.10) | collective-permute-done | bytes 262176 | tf_op jit(solution)/shard_map/ppermute | solution.py:22
  81.0 1.4 %collective-permute-done.8 = bf16[4,128,256]{2,1,0:T(8,128)(2,1)S(1)} collective-permute-done((bf16[4,128,256]{2,1,0:T(8,128)(2,1)S(1)}, bf16[4,128,256]{2,1,0:T(8,128)(2,1)S(1)}, u32[]{:S(2)}, u32[]{:S(2)}) %collective-permute-start.8) | collective-permute-done | bytes 262176 | tf_op jit(solution)/shard_map/ppermute | solution.py:22
  82.5 0.4 collective-permute-start.11
  82.9 5.4 %grads.1 = (f32[1024,512]{1,0:T(8,128)}, f32[1,1024]{1,0:T(1,128)}) custom-call(s32[1]{0:T(128)} %bitcast.7.me_ref, bf16[4,192,1024]{2,1,0:T(8,128)(2,1)} %get-tuple-element.103.x_ref, bf16[1,1024]{1,0:T(2,128)(2,1)S(1)} %copy-done.6, bf16[1024,512]{1,0:T(8,128)(2,1)} %get-tuple-element.97.refs_4_.weight_ref, ...), custom_call_target="tpu_custom_call" | custom-call | flops 2147483648 | bytes 4194304 | tf_op jit(solution)/shard_map/grads/pallas_call | solution.py:297
  88.4 1.5 %collective-permute-done.11 = bf16[128,512]{1,0:T(8,128)(2,1)S(1)} collective-permute-done((bf16[128,512]{1,0:T(8,128)(2,1)S(1)}, bf16[128,512]{1,0:T(8,128)(2,1)S(1)}, u32[]{:S(2)}, u32[]{:S(2)}) %collective-permute-start.11) | collective-permute-done | bytes 131104 | tf_op jit(solution)/shard_map/ppermute | solution.py:22
  89.8 0.7 fusion
  (49 shorter events, 0.7 us)
Async XLA Ops:
  0.6 13.3 %copy-start.6 = (bf16[1,1024]{1,0:T(2,128)(2,1)S(1)}, bf16[1,1024]{1,0:T(2,128)(2,1)}, u32[]{:S(2)}) copy-start(bf16[1,1024]{1,0:T(2,128)(2,1)} %gain_ref.1) | copy-start | bytes 6148
  0.6 1.6 %copy-start = (bf16[1,128,8192]{2,1,0:T(8,128)(2,1)S(1)}, bf16[1,128,8192]{2,1,0:T(8,128)(2,1)}, u32[]{:S(2)}) copy-start(bf16[1,128,8192]{2,1,0:T(8,128)(2,1)} %param.15) | copy-start | bytes 6291460
  2.2 2.6 %copy-start.5 = (bf16[1,128,512]{2,1,0:T(8,128)(2,1)S(1)}, bf16[1,128,512]{2,1,0:T(8,128)(2,1)}, u32[]{:S(2)}) copy-start(bf16[1,128,512]{2,1,0:T(8,128)(2,1)} %param.17) | copy-start | bytes 393220
  4.9 57.3 %collective-permute-start.5 = (bf16[192,1024]{1,0:T(8,128)(2,1)S(1)}, bf16[192,1024]{1,0:T(8,128)(2,1)S(1)}, u32[]{:S(2)}, u32[]{:S(2)}) collective-permute-start(bf16[192,1024]{1,0:T(8,128)(2,1)S(1)} %get-tuple-element.126), channel_id=1, source_target_pairs={{0,6},{1,7},{2,4},{3,5},{4,2},{5,3},{6,0},{7,1},{8,14},{9,15},{10,... | collective-permute-start | bytes 1179656 | tf_op jit(solution)/shard_map/ppermute | solution.py:22
  10.0 52.2 %collective-permute-start.3 = (bf16[128,1024]{1,0:T(8,128)(2,1)S(1)}, bf16[128,1024]{1,0:T(8,128)(2,1)S(1)}, u32[]{:S(2)}, u32[]{:S(2)}) collective-permute-start(bf16[128,1024]{1,0:T(8,128)(2,1)S(1)} %get-tuple-element.93), channel_id=1, source_target_pairs={{0,4},{1,5},{2,6},{3,7},{4,0},{5,1},{6,2},{7,3},{8,12},{9,13},{10,... | collective-permute-start | bytes 786440 | tf_op jit(solution)/shard_map/ppermute | solution.py:22
  10.0 52.2 %collective-permute-start.4 = (bf16[128,1024]{1,0:T(8,128)(2,1)S(1)}, bf16[128,1024]{1,0:T(8,128)(2,1)S(1)}, u32[]{:S(2)}, u32[]{:S(2)}) collective-permute-start(bf16[128,1024]{1,0:T(8,128)(2,1)S(1)} %get-tuple-element.94), channel_id=1, source_target_pairs={{0,5},{1,4},{2,7},{3,6},{4,1},{5,0},{6,3},{7,2},{8,13},{9,12},{10,... | collective-permute-start | bytes 786440 | tf_op jit(solution)/shard_map/ppermute | solution.py:22
  13.9 48.3 %collective-permute-start.6 = (bf16[128,1024]{1,0:T(8,128)(2,1)S(1)}, bf16[128,1024]{1,0:T(8,128)(2,1)S(1)}, u32[]{:S(2)}, u32[]{:S(2)}) collective-permute-start(bf16[128,1024]{1,0:T(8,128)(2,1)S(1)} %get-tuple-element.96), channel_id=1, source_target_pairs={{0,7},{1,6},{2,5},{3,4},{4,3},{5,2},{6,1},{7,0},{8,15},{9,14},{10,... | collective-permute-start | bytes 786440 | tf_op jit(solution)/shard_map/ppermute | solution.py:22
  13.9 2.9 %copy-start.3 = (bf16[4,128,1024]{2,1,0:T(8,128)(2,1)S(1)}, bf16[4,128,1024]{2,1,0:T(8,128)(2,1)}, u32[]{:S(2)}) copy-start(bf16[4,128,1024]{2,1,0:T(8,128)(2,1)} %get-tuple-element.46) | copy-start | bytes 3145732 | tf_op jit(solution)/shard_map/cond
  16.7 8.8 %collective-permute-start = (bf16[2048,128]{1,0:T(8,128)(2,1)S(1)}, bf16[2048,128]{1,0:T(8,128)(2,1)S(1)}, u32[]{:S(2)}, u32[]{:S(2)}) collective-permute-start(bf16[2048,128]{1,0:T(8,128)(2,1)S(1)} %decode.3), channel_id=1, source_target_pairs={{0,8},{8,0},{16,24},{24,16},{1,9},{9,1},{17,25},{25,17},{2,10},{10... | collective-permute-start | bytes 1572872 | tf_op jit(solution)/shard_map/cond/branch_1_fun/ppermute | solution.py:22
  18.1 4.5 %copy-start.4 = (f32[1,8192]{1,0:T(1,128)S(1)}, f32[1,8192]{1,0:T(1,128)}, u32[]{:S(2)}) copy-start(f32[1,8192]{1,0:T(1,128)} %get-tuple-element.111) | copy-start | bytes 98308 | tf_op jit(solution)/shard_map/cond
  18.1 41.6 %all-to-all-start = ((bf16[4,192,1024]{2,1,0:T(8,128)(2,1)}), bf16[4,192,1024]{2,1,0:T(8,128)(2,1)}, u32[]{:S(2)}, u32[]{:S(2)}) async-start(bf16[4,192,1024]{2,1,0:T(8,128)(2,1)} %pad_maximum_fusion), calls=%async_computation | async-start | bytes 3145728 | tf_op jit(solution)/shard_map/cond/branch_1_fun/all_to_all | solution.py:370
  22.6 19.5 %copy-start.2 = (f32[524288]{0:T(1024)S(1)}, f32[524288]{0:T(1024)}, u32[]{:S(2)}) copy-start(f32[524288]{0:T(1024)} %get-tuple-element.113) | copy-start | bytes 6291460 | tf_op jit(solution)/shard_map/cond
  25.5 16.7 %copy-start.1 = (f32[524288]{0:T(1024)S(1)}, f32[524288]{0:T(1024)}, u32[]{:S(2)}) copy-start(f32[524288]{0:T(1024)} %get-tuple-element.112) | copy-start | bytes 6291460 | tf_op jit(solution)/shard_map/cond
  25.6 14.4 %collective-permute-start.1 = (bf16[2048,128]{1,0:T(8,128)(2,1)S(1)}, bf16[2048,128]{1,0:T(8,128)(2,1)S(1)}, u32[]{:S(2)}, u32[]{:S(2)}) collective-permute-start(bf16[2048,128]{1,0:T(8,128)(2,1)S(1)} %add_convert_fusion.1), channel_id=1, source_target_pairs={{0,16},{8,24},{16,0},{24,8},{1,17},{9,25},{17,1},{25,9},{2,18},{10... | collective-permute-start | bytes 1572872 | tf_op jit(solution)/shard_map/cond/branch_1_fun/ppermute | solution.py:22
  40.2 2.0 %collective-permute-start.2 = (bf16[2048,128]{1,0:T(8,128)(2,1)S(1)}, bf16[2048,128]{1,0:T(8,128)(2,1)S(1)}, u32[]{:S(2)}, u32[]{:S(2)}) collective-permute-start(bf16[2048,128]{1,0:T(8,128)(2,1)S(1)} %add_convert_fusion.mine_ref), channel_id=1, source_target_pairs={{0,8},{8,0},{16,24},{24,16},{1,9},{9,1},{17,25},{25,17},{2,10},{10... | collective-permute-start | bytes 1572872 | tf_op jit(solution)/shard_map/cond/branch_1_fun/ppermute | solution.py:22
  64.3 9.4 %collective-permute-start.9 = (bf16[5,128,256]{2,1,0:T(8,128)(2,1)S(1)}, bf16[5,128,256]{2,1,0:T(8,128)(2,1)S(1)}, u32[]{:S(2)}, u32[]{:S(2)}) collective-permute-start(bf16[5,128,256]{2,1,0:T(8,128)(2,1)S(1)} %pad_maximum_fusion.2), channel_id=1, source_target_pairs={{0,2},{1,3},{2,0},{3,1},{4,6},{5,7},{6,4},{7,5},{8,10},{9,11},{10,... | collective-permute-start | bytes 983048 | tf_op jit(solution)/shard_map/ppermute | solution.py:22
  64.4 10.9 %collective-permute-start.7 = (bf16[5,128,256]{2,1,0:T(8,128)(2,1)S(1)}, bf16[5,128,256]{2,1,0:T(8,128)(2,1)S(1)}, u32[]{:S(2)}, u32[]{:S(2)}) collective-permute-start(bf16[5,128,256]{2,1,0:T(8,128)(2,1)S(1)} %pad_maximum_fusion.1), channel_id=1, source_target_pairs={{0,1},{1,0},{2,3},{3,2},{4,5},{5,4},{6,7},{7,6},{8,9},{9,8},{10,11... | collective-permute-start | bytes 983048 | tf_op jit(solution)/shard_map/ppermute | solution.py:22
  73.8 7.1 %collective-permute-start.10 = (bf16[4,128,256]{2,1,0:T(8,128)(2,1)S(1)}, bf16[4,128,256]{2,1,0:T(8,128)(2,1)S(1)}, u32[]{:S(2)}, u32[]{:S(2)}) collective-permute-start(bf16[4,128,256]{2,1,0:T(8,128)(2,1)S(1)} %pad_maximum_fusion.4), channel_id=1, source_target_pairs={{0,1},{1,0},{2,3},{3,2},{4,5},{5,4},{6,7},{7,6},{8,9},{9,8},{10,11... | collective-permute-start | bytes 786440 | tf_op jit(solution)/shard_map/ppermute | solution.py:22
  75.5 6.8 %collective-permute-start.8 = (bf16[4,128,256]{2,1,0:T(8,128)(2,1)S(1)}, bf16[4,128,256]{2,1,0:T(8,128)(2,1)S(1)}, u32[]{:S(2)}, u32[]{:S(2)}) collective-permute-start(bf16[4,128,256]{2,1,0:T(8,128)(2,1)S(1)} %pad_maximum_fusion.3), channel_id=1, source_target_pairs={{0,2},{1,3},{2,0},{3,1},{4,6},{5,7},{6,4},{7,5},{8,10},{9,11},{10,... | collective-permute-start | bytes 786440 | tf_op jit(solution)/shard_map/ppermute | solution.py:22
  82.5 7.3 %collective-permute-start.11 = (bf16[128,512]{1,0:T(8,128)(2,1)S(1)}, bf16[128,512]{1,0:T(8,128)(2,1)S(1)}, u32[]{:S(2)}, u32[]{:S(2)}) collective-permute-start(bf16[128,512]{1,0:T(8,128)(2,1)S(1)} %pad_maximum_fusion.8), channel_id=1, source_target_pairs={{0,4},{1,5},{2,6},{3,7},{4,0},{5,1},{6,2},{7,3},{8,12},{9,13},{10,... | collective-permute-start | bytes 393224 | tf_op jit(solution)/shard_map/ppermute | solution.py:22

commit v2 on v1

--- a/solution.py
+++ b/solution.py
@@ -181,58 +181,40 @@
         out_ref[order.index(slot)] = part[:, at * cut : (at + 1) * cut]
 
 
-def near_keys_kernel(orders, me_ref, x_ref, weight_ref, gain_ref, *out_refs):
+def keys_kernel(orders, me_ref, columns_ref, *refs):
+    cuts = len(orders)
+    *x_refs, weight_ref, gain_ref = refs[: -2 * cuts]
+    near_refs, far_refs = refs[-2 * cuts : -cuts], refs[-cuts:]
     gain = gain_ref[...].astype(jnp.float32)
     weight = weight_ref[...]
-    near, tokens, _ = out_refs[0].shape
-    for slot in range(near):
-        x = x_ref[(me_ref[0] & (near - 1)) ^ slot, x_ref.shape[1] - tokens :, :]
-        normed = (x.astype(jnp.float32) * gain).astype(jnp.bfloat16)
-        part = jnp.dot(normed, weight, preferred_element_type=jnp.float32).astype(jnp.bfloat16)
-        store_cuts(out_refs, orders, slot, part)
-
-
-def near_partial_keys(columns, me, tokens, orders, weight, gain):
-    near, _, width = columns.shape
-    key_width = weight.shape[1]
-    flops = 2 * near * tokens * width * key_width
+    near, tokens, _ = near_refs[0].shape
+    for out_refs in (far_refs, near_refs):
+        for slot in range(near):
+            if out_refs is far_refs:
+                x = x_refs[slot][x_refs[slot].shape[0] - tokens :, :]
+            else:
+                x = columns_ref[(me_ref[0] & (near - 1)) ^ slot, columns_ref.shape[1] - tokens :, :]
+            normed = (x.astype(jnp.float32) * gain).astype(jnp.bfloat16)
+            part = jnp.dot(normed, weight, preferred_element_type=jnp.float32).astype(jnp.bfloat16)
+            store_cuts(out_refs, orders, slot, part)
+
+
+def partial_keys(columns, blocks, me, tokens, orders, weight, gain):
+    width, key_width = weight.shape
+    near = len(blocks)
+    flops = 4 * near * tokens * width * key_width
     whole = pl.BlockSpec(memory_space=pltpu.VMEM)
     cut = jax.ShapeDtypeStruct((near, tokens, key_width // len(orders)), jnp.bfloat16)
-    return pl.pallas_call(
-        functools.partial(near_keys_kernel, orders),
-        in_specs=[pl.BlockSpec(memory_space=pltpu.SMEM), whole, whole, whole],
-        out_specs=[whole] * len(orders),
-        out_shape=[cut] * len(orders),
+    parts = pl.pallas_call(
+        functools.partial(keys_kernel, orders),
+        in_specs=[pl.BlockSpec(memory_space=pltpu.SMEM)] + [whole] * (near + 3),
+        out_specs=[whole] * (2 * len(orders)),
+        out_shape=[cut] * (2 * len(orders)),
         compiler_params=params(),
         cost_estimate=pl.CostEstimate(flops=flops, bytes_accessed=flops // 256, transcendentals=0),
-        name="near_partial_keys",
-    )(me, columns, weight, gain)
-
-
-def far_keys_kernel(orders, *refs):
-    *x_refs, weight_ref, gain_ref = refs[: -len(orders)]
-    out_refs = refs[-len(orders) :]
-    gain = gain_ref[...].astype(jnp.float32)
-    weight = weight_ref[...]
-    tokens = out_refs[0].shape[1]
-    for slot, x_ref in enumerate(x_refs):
-        x = x_ref[x_ref.shape[0] - tokens :, :]
-        normed = (x.astype(jnp.float32) * gain).astype(jnp.bfloat16)
-        part = jnp.dot(normed, weight, preferred_element_type=jnp.float32).astype(jnp.bfloat16)
-        store_cuts(out_refs, orders, slot, part)
-
-
-def far_partial_keys(blocks, tokens, orders, weight, gain):
-    width, key_width = weight.shape
-    flops = 2 * len(blocks) * tokens * width * key_width
-    cut = jax.ShapeDtypeStruct((len(blocks), tokens, key_width // len(orders)), jnp.bfloat16)
-    return pl.pallas_call(
-        functools.partial(far_keys_kernel, orders),
-        out_shape=[cut] * len(orders),
-        compiler_params=params(),
-        cost_estimate=pl.CostEstimate(flops=flops, bytes_accessed=flops // 256, transcendentals=0),
-        name="far_partial_keys",
-    )(*blocks, weight, gain)
+        name="partial_keys",
+    )(me, columns, *blocks, weight, gain)
+    return parts[: len(orders)], parts[len(orders) :]
 
 
 def by_bits(count, bits):
@@ -365,15 +347,14 @@
     swapped = [bits[1], bits[0]] + bits[2:]
     orders = [by_bits(far, each) for each in (bits, swapped)]
 
-    def beside(codes, scales, base, momentum, near, packed, gain):
+    def beside(codes, scales, base, momentum, near, packed):
         near = jnp.concatenate([jnp.broadcast_to(packed, (far, *packed.shape)), near], axis=1)
         columns = lax.all_to_all(near, "fsdp", split_axis=0, concat_axis=0, tiled=True, axis_index_groups=halves)
         mine, other = sum_over_replicas(codes, scales, core)
         updated = update(mine, other, core, base, momentum, replicas, key_width)
-        weight = updated[-1]
-        return *updated, columns, *near_partial_keys(columns, me, tokens, orders, weight, gain)
-
-    new_base, new_momentum, weight, columns, *near_parts = stage(
+        return *updated, columns
+
+    new_base, new_momentum, weight, columns = stage(
         beside,
         codes.reshape(-1, LANES),
         scales.reshape(-1, LANES),
@@ -381,12 +362,11 @@
         momentum.reshape(-1, LANES),
         near,
         packed,
-        gain,
     )
 
     rider = far_blocks[RIDER]
     far_tokens = jnp.split(unpack(rider[: rider.shape[0] - tokens], tokens, key_width)[None], 2, axis=2)
-    far_parts = far_partial_keys(far_blocks, tokens, orders, weight, gain)
+    near_parts, far_parts = partial_keys(columns, far_blocks, me, tokens, orders, weight, gain)
     folded = [fold(*each) for each in zip(near_parts, far_parts, (bits, swapped), far_tokens)]
     own, given, spread = zip(*folded)
     given, columns, *spread = lax.optimization_barrier((jnp.concatenate(given, axis=1), columns, *spread))

time: 91.1 us -> 89.9 us (0.987)
  Pallas kernels: 21 us -> 19.6 us
  waiting for transfers between devices: 44.8 us -> 43.4 us
  starting transfers between devices: 19.3 us -> 20.3 us
    ppermute x12, waiting for transfers between devices: 30.2 us -> 28.8 us  [swap(): lax.ppermute(value, axis, [(i, i ^ bit) for i in range(lax.axis_size(axis...]
    pallas_call x2 -> x1, Pallas kernels: 4.37 us -> 3 us  [partial_keys(): pl.pallas_call(functools.partial(keys_kernel, orders), in_specs=[pl.Block...]
    ppermute x12, starting transfers between devices: 14.8 us -> 15.8 us  [swap(): lax.ppermute(value, axis, [(i, i ^ bit) for i in range(lax.axis_size(axis...]
  transfers between devices with their start and end apart: 13 -> 13, of which waited for: 7 -> 7; matrix products, arithmetic and copies ran while one was open for 2% -> 2% of each run, Pallas kernels for 18% -> 16%
where the time goes in v2:
time: 89.9 us; the launch traced here: 89.4 us
  waiting for transfers between devices  43.4 us (48%)
  starting transfers between devices  20.3 us (23%)
  Pallas kernels  19.6 us (22%)
  other arithmetic  2.71 us (3%)
  local copies, waits for them, and re-layouts  2.4 us (3%)
    ppermute x12, waiting for transfers between devices, swap(): lax.ppermute(value, axis, [(i, i ^ bit) for i in range(lax.axis_size(axis...  28.8 us
    ppermute x12, starting transfers between devices, swap(): lax.ppermute(value, axis, [(i, i ^ bit) for i in range(lax.axis_size(axis...  15.8 us
    all_to_all x1, waiting for transfers between devices, beside(): lax.all_to_all(near, 'fsdp', split_axis=0, concat_axis=0, tiled=True, axi...  14.6 us
    pallas_call x2, Pallas kernels, decode(): pl.pallas_call(decode_kernel, grid_spec=pltpu.PrefetchScalarGridSpec(num_...  5.49 us
    pallas_call x1, Pallas kernels, grads(): pl.pallas_call(functools.partial(grads_kernel, orders), grid_spec=pltpu.P...  5.47 us
    all_to_all x1, starting transfers between devices, beside(): lax.all_to_all(near, 'fsdp', split_axis=0, concat_axis=0, tiled=True, axi...  4.47 us
    pallas_call x1, Pallas kernels, partial_keys(): pl.pallas_call(functools.partial(keys_kernel, orders), in_specs=[pl.Block...  3 us
    pallas_call x1, Pallas kernels, update(): pl.pallas_call(functools.partial(update_kernel, replicas), grid_spec=pltp...  2.96 us
  transfers between devices with their start and end apart: 13, of which 7 were waited for; matrix products, arithmetic and copies ran while one was open for 2% of the time, Pallas kernels for 16%

profile of v2, /device:TPU:0, one launch (start us, length us, event | category | flops | bytes accessed | tf_op | source)
XLA Modules:
  0.0 89.4 jit_solution(7824144090898472948)
XLA Ops:
  0.6 1.6 %copy-done = bf16[1,128,8192]{2,1,0:T(8,128)(2,1)S(1)} copy-done((bf16[1,128,8192]{2,1,0:T(8,128)(2,1)S(1)}, bf16[1,128,8192]{2,1,0:T(8,128)(2,1)}, u32[]{:S(2)}) %copy-start) | copy-done | bytes 2097176
  2.2 2.6 %scale_inputs.1 = (bf16[4,128,1024]{2,1,0:T(8,128)(2,1)}, bf16[128,1024]{1,0:T(8,128)(2,1)S(1)}, bf16[128,1024]{1,0:T(8,128)(2,1)S(1)}, bf16[192,1024]{1,0:T(8,128)(2,1)S(1)}, bf16[128,1024]{1,0:T(8,128)(2,1)S(1)}) custom-call(s32[1]{0:T(128)} %bitcast.7.me_ref, bf16[128,8192]{1,0:T(8,128)(2,1)S(1)} %bitcast.26), custom_call_target="tpu_custom_call" | custom-call | flops 4194304 | bytes 4194304 | tf_op jit(solution)/shard_map/scale_inputs/pallas_call | solution.py:76
  4.9 5.1 %collective-permute-start.5 = (bf16[192,1024]{1,0:T(8,128)(2,1)S(1)}, bf16[192,1024]{1,0:T(8,128)(2,1)S(1)}, u32[]{:S(2)}, u32[]{:S(2)}) collective-permute-start(bf16[192,1024]{1,0:T(8,128)(2,1)S(1)} %get-tuple-element.118), channel_id=1, source_target_pairs={{0,6},{1,7},{2,4},{3,5},{4,2},{5,3},{6,0},{7,1},{8,14},{9,15},{10,... | collective-permute-start | bytes 1179656 | tf_op jit(solution)/shard_map/ppermute | solution.py:22
  10.0 3.8 %collective-permute-start.4 = (bf16[128,1024]{1,0:T(8,128)(2,1)S(1)}, bf16[128,1024]{1,0:T(8,128)(2,1)S(1)}, u32[]{:S(2)}, u32[]{:S(2)}) collective-permute-start(bf16[128,1024]{1,0:T(8,128)(2,1)S(1)} %get-tuple-element.86), channel_id=1, source_target_pairs={{0,5},{1,4},{2,7},{3,6},{4,1},{5,0},{6,3},{7,2},{8,13},{9,12},{10,... | collective-permute-start | bytes 786440 | tf_op jit(solution)/shard_map/ppermute | solution.py:22
  13.9 46.3 %conditional.1 = (bf16[1024,512]{1,0:T(8,128)(2,1)}, bf16[4,192,1024]{2,1,0:T(8,128)(2,1)}, f32[524288]{0:T(1024)}, f32[524288]{0:T(1024)}) conditional(s32[]{:T(128)} %convert_element_type.102, () %tuple.27, (s32[]{:T(128)}, s32[1,524288]{1,0:T(1,128)}, f32[1,8192]{1,0:T(1,128)S(1)}, f32[524288]{0:T(1024)}, f32[524288]{0:T(1024)}, ...), branch_computations={%region_0.0_spmd, %region_1.0_spmd} | conditional | flops 9437186 | bytes 52822364 | solution.py:324
  14.0 0.6 copy-done.6
  14.6 2.7 %decode.3 = bf16[2048,128]{1,0:T(8,128)(2,1)S(1)} custom-call(s32[1]{0:T(128)S(6)} %sub.2.half_ref, s32[4096,128]{1,0:T(8,128)} %bitcast.27, f32[64,128]{1,0:T(8,128)S(1)} %bitcast.31), custom_call_target="tpu_custom_call" | custom-call | flops 524288 | bytes 1572864 | tf_op jit(solution)/shard_map/cond/branch_1_fun/decode/pallas_call | solution.py:120
  17.2 0.1 collective-permute-start
  17.4 1.3 %pad_maximum_fusion = bf16[4,192,1024]{2,1,0:T(8,128)(2,1)} fusion(bf16[4,128,1024]{2,1,0:T(8,128)(2,1)S(1)} %copy-done.4, bf16[4,64,1024]{2,1,0:T(8,128)(2,1)S(1)} %broadcast_in_dim.14), kind=kLoop, calls=%fused_computation | loop fusion | flops 3145728 | bytes 3145728 | tf_op jit(solution)/shard_map/cond/branch_1_fun/concatenate | solution.py:351
  18.7 4.5 %all-to-all-start = ((bf16[4,192,1024]{2,1,0:T(8,128)(2,1)}), bf16[4,192,1024]{2,1,0:T(8,128)(2,1)}, u32[]{:S(2)}, u32[]{:S(2)}) async-start(bf16[4,192,1024]{2,1,0:T(8,128)(2,1)} %pad_maximum_fusion), calls=%async_computation | async-start | bytes 3145728 | tf_op jit(solution)/shard_map/cond/branch_1_fun/all_to_all | solution.py:352
  23.2 2.8 %decode.2 = bf16[2048,128]{1,0:T(8,128)(2,1)S(1)} custom-call(s32[1]{0:T(128)} %bitcast.half_ref.core_ref, s32[4096,128]{1,0:T(8,128)} %bitcast.28, f32[64,128]{1,0:T(8,128)S(1)} %bitcast.32), custom_call_target="tpu_custom_call" | custom-call | flops 524288 | bytes 1572864 | tf_op jit(solution)/shard_map/cond/branch_1_fun/decode/pallas_call | solution.py:120
  26.0 0.1 add_convert_fusion.1
  26.2 1.7 %collective-permute-start.1 = (bf16[2048,128]{1,0:T(8,128)(2,1)S(1)}, bf16[2048,128]{1,0:T(8,128)(2,1)S(1)}, u32[]{:S(2)}, u32[]{:S(2)}) collective-permute-start(bf16[2048,128]{1,0:T(8,128)(2,1)S(1)} %add_convert_fusion.1), channel_id=1, source_target_pairs={{0,16},{8,24},{16,0},{24,8},{1,17},{9,25},{17,1},{25,9},{2,18},{10... | collective-permute-start | bytes 1572872 | tf_op jit(solution)/shard_map/cond/branch_1_fun/ppermute | solution.py:22
  27.9 12.7 %collective-permute-done.1 = bf16[2048,128]{1,0:T(8,128)(2,1)S(1)} collective-permute-done((bf16[2048,128]{1,0:T(8,128)(2,1)S(1)}, bf16[2048,128]{1,0:T(8,128)(2,1)S(1)}, u32[]{:S(2)}, u32[]{:S(2)}) %collective-permute-start.1) | collective-permute-done | bytes 524320 | tf_op jit(solution)/shard_map/cond/branch_1_fun/ppermute | solution.py:22
  40.5 0.1 add_convert_fusion.mine_ref
  40.7 0.1 collective-permute-start.2
  40.8 1.9 %collective-permute-done.2.other_ref = bf16[2048,128]{1,0:T(8,128)(2,1)S(1)} collective-permute-done((bf16[2048,128]{1,0:T(8,128)(2,1)S(1)}, bf16[2048,128]{1,0:T(8,128)(2,1)S(1)}, u32[]{:S(2)}, u32[]{:S(2)}) %collective-permute-start.2) | collective-permute-done | bytes 524320 | tf_op jit(solution)/shard_map/cond/branch_1_fun/ppermute | solution.py:22
  42.7 3.0 %update.1 = (f32[4096,128]{1,0:T(8,128)}, f32[4096,128]{1,0:T(8,128)}, bf16[1024,512]{1,0:T(8,128)(2,1)}) custom-call(s32[1]{0:T(128)} %bitcast.half_ref.core_ref, bf16[2048,128]{1,0:T(8,128)(2,1)S(1)} %add_convert_fusion.mine_ref, bf16[2048,128]{1,0:T(8,128)(2,1)S(1)} %collective-permute-done.2.other_ref, f32[4096,128]{1,0:T(8,128)S(1)} %bitcast.29, ...), custom_call_target="tpu_custom_call" | custom-call | flops 3145728 | bytes 10485760 | tf_op jit(solution)/shard_map/cond/branch_1_fun/update/pallas_call | solution.py:159
  45.6 14.6 %all-to-all-done = bf16[4,192,1024]{2,1,0:T(8,128)(2,1)} async-done(((bf16[4,192,1024]{2,1,0:T(8,128)(2,1)}), bf16[4,192,1024]{2,1,0:T(8,128)(2,1)}, u32[]{:S(2)}, u32[]{:S(2)}) %all-to-all-start) | async-done | bytes 1572896 | tf_op jit(solution)/shard_map/cond/branch_1_fun/all_to_all | solution.py:352
  60.3 3.0 %partial_keys.1 = (bf16[4,128,256]{2,1,0:T(8,128)(2,1)S(1)}, bf16[4,128,256]{2,1,0:T(8,128)(2,1)S(1)}, bf16[4,128,256]{2,1,0:T(8,128)(2,1)S(1)}, bf16[4,128,256]{2,1,0:T(8,128)(2,1)S(1)}) custom-call(s32[1]{0:T(128)} %bitcast.7.me_ref, bf16[4,192,1024]{2,1,0:T(8,128)(2,1)} %get-tuple-element.95.columns_ref.x_ref, ...), custom_call_target="tpu_custom_call" | custom-call | flops 1073741824 | bytes 4194304 | tf_op jit(solution)/shard_map/partial_keys/pallas_call | solution.py:208
  63.4 1.8 %collective-permute-start.9 = (bf16[5,128,256]{2,1,0:T(8,128)(2,1)S(1)}, bf16[5,128,256]{2,1,0:T(8,128)(2,1)S(1)}, u32[]{:S(2)}, u32[]{:S(2)}) collective-permute-start(bf16[5,128,256]{2,1,0:T(8,128)(2,1)S(1)} %pad_maximum_fusion.2), channel_id=1, source_target_pairs={{0,2},{1,3},{2,0},{3,1},{4,6},{5,7},{6,4},{7,5},{8,10},{9,11},{10,... | collective-permute-start | bytes 983048 | tf_op jit(solution)/shard_map/ppermute | solution.py:22
  65.3 0.6 collective-permute-start.7
  65.9 7.0 %collective-permute-done.9 = bf16[5,128,256]{2,1,0:T(8,128)(2,1)S(1)} collective-permute-done((bf16[5,128,256]{2,1,0:T(8,128)(2,1)S(1)}, bf16[5,128,256]{2,1,0:T(8,128)(2,1)S(1)}, u32[]{:S(2)}, u32[]{:S(2)}) %collective-permute-start.9) | collective-permute-done | bytes 327712 | tf_op jit(solution)/shard_map/ppermute | solution.py:22
  72.8 0.1 add_convert_fusion.4
  73.0 1.5 %collective-permute-start.10 = (bf16[4,128,256]{2,1,0:T(8,128)(2,1)S(1)}, bf16[4,128,256]{2,1,0:T(8,128)(2,1)S(1)}, u32[]{:S(2)}, u32[]{:S(2)}) collective-permute-start(bf16[4,128,256]{2,1,0:T(8,128)(2,1)S(1)} %pad_maximum_fusion.4), channel_id=1, source_target_pairs={{0,1},{1,0},{2,3},{3,2},{4,5},{5,4},{6,7},{7,6},{8,9},{9,8},{10,11... | collective-permute-start | bytes 786440 | tf_op jit(solution)/shard_map/ppermute | solution.py:22
  74.7 0.4 collective-permute-start.8
  75.0 5.1 %collective-permute-done.10 = bf16[4,128,256]{2,1,0:T(8,128)(2,1)S(1)} collective-permute-done((bf16[4,128,256]{2,1,0:T(8,128)(2,1)S(1)}, bf16[4,128,256]{2,1,0:T(8,128)(2,1)S(1)}, u32[]{:S(2)}, u32[]{:S(2)}) %collective-permute-start.10) | collective-permute-done | bytes 262176 | tf_op jit(solution)/shard_map/ppermute | solution.py:22
  80.1 1.3 %collective-permute-done.8 = bf16[4,128,256]{2,1,0:T(8,128)(2,1)S(1)} collective-permute-done((bf16[4,128,256]{2,1,0:T(8,128)(2,1)S(1)}, bf16[4,128,256]{2,1,0:T(8,128)(2,1)S(1)}, u32[]{:S(2)}, u32[]{:S(2)}) %collective-permute-start.8) | collective-permute-done | bytes 262176 | tf_op jit(solution)/shard_map/ppermute | solution.py:22
  81.6 0.7 collective-permute-start.11
  82.4 5.5 %grads.1 = (f32[1024,512]{1,0:T(8,128)}, f32[1,1024]{1,0:T(1,128)}) custom-call(s32[1]{0:T(128)} %bitcast.7.me_ref, bf16[4,192,1024]{2,1,0:T(8,128)(2,1)} %get-tuple-element.95.columns_ref.x_ref, bf16[1,1024]{1,0:T(2,128)(2,1)S(1)} %copy-done.1, bf16[1024,512]{1,0:T(8,128)(2,1)} %get-tuple-element.89.refs_4_.weight_ref, ...), custom_call_target="tpu_custom_call" | custom-call | flops 2147483648 | bytes 4194304 | tf_op jit(solution)/shard_map/grads/pallas_call | solution.py:279
  87.8 0.9 collective-permute-done.11
  88.7 0.7 fusion
  (52 shorter events, 0.7 us)
Async XLA Ops:
  0.6 1.6 %copy-start = (bf16[1,128,8192]{2,1,0:T(8,128)(2,1)S(1)}, bf16[1,128,8192]{2,1,0:T(8,128)(2,1)}, u32[]{:S(2)}) copy-start(bf16[1,128,8192]{2,1,0:T(8,128)(2,1)} %param.15) | copy-start | bytes 6291460
  2.2 2.6 %copy-start.8 = (bf16[1,128,512]{2,1,0:T(8,128)(2,1)S(1)}, bf16[1,128,512]{2,1,0:T(8,128)(2,1)}, u32[]{:S(2)}) copy-start(bf16[1,128,512]{2,1,0:T(8,128)(2,1)} %param.17) | copy-start | bytes 393220
  2.2 11.7 %copy-start.5 = (f32[1,8192]{1,0:T(1,128)S(1)}, f32[1,8192]{1,0:T(1,128)}, u32[]{:S(2)}) copy-start(f32[1,8192]{1,0:T(1,128)} %param.12) | copy-start | bytes 98308
  4.9 55.3 %collective-permute-start.5 = (bf16[192,1024]{1,0:T(8,128)(2,1)S(1)}, bf16[192,1024]{1,0:T(8,128)(2,1)S(1)}, u32[]{:S(2)}, u32[]{:S(2)}) collective-permute-start(bf16[192,1024]{1,0:T(8,128)(2,1)S(1)} %get-tuple-element.118), channel_id=1, source_target_pairs={{0,6},{1,7},{2,4},{3,5},{4,2},{5,3},{6,0},{7,1},{8,14},{9,15},{10,... | collective-permute-start | bytes 1179656 | tf_op jit(solution)/shard_map/ppermute | solution.py:22
  10.0 50.2 %collective-permute-start.3 = (bf16[128,1024]{1,0:T(8,128)(2,1)S(1)}, bf16[128,1024]{1,0:T(8,128)(2,1)S(1)}, u32[]{:S(2)}, u32[]{:S(2)}) collective-permute-start(bf16[128,1024]{1,0:T(8,128)(2,1)S(1)} %get-tuple-element.85), channel_id=1, source_target_pairs={{0,4},{1,5},{2,6},{3,7},{4,0},{5,1},{6,2},{7,3},{8,12},{9,13},{10,... | collective-permute-start | bytes 786440 | tf_op jit(solution)/shard_map/ppermute | solution.py:22
  10.0 50.2 %collective-permute-start.4 = (bf16[128,1024]{1,0:T(8,128)(2,1)S(1)}, bf16[128,1024]{1,0:T(8,128)(2,1)S(1)}, u32[]{:S(2)}, u32[]{:S(2)}) collective-permute-start(bf16[128,1024]{1,0:T(8,128)(2,1)S(1)} %get-tuple-element.86), channel_id=1, source_target_pairs={{0,5},{1,4},{2,7},{3,6},{4,1},{5,0},{6,3},{7,2},{8,13},{9,12},{10,... | collective-permute-start | bytes 786440 | tf_op jit(solution)/shard_map/ppermute | solution.py:22
  13.9 46.4 %collective-permute-start.6 = (bf16[128,1024]{1,0:T(8,128)(2,1)S(1)}, bf16[128,1024]{1,0:T(8,128)(2,1)S(1)}, u32[]{:S(2)}, u32[]{:S(2)}) collective-permute-start(bf16[128,1024]{1,0:T(8,128)(2,1)S(1)} %get-tuple-element.88), channel_id=1, source_target_pairs={{0,7},{1,6},{2,5},{3,4},{4,3},{5,2},{6,1},{7,0},{8,15},{9,14},{10,... | collective-permute-start | bytes 786440 | tf_op jit(solution)/shard_map/ppermute | solution.py:22
  13.9 46.3 %copy-start.1 = (bf16[1,1024]{1,0:T(2,128)(2,1)S(1)}, bf16[1,1024]{1,0:T(2,128)(2,1)}, u32[]{:S(2)}) copy-start(bf16[1,1024]{1,0:T(2,128)(2,1)} %gain_ref.1) | copy-start | bytes 6148
  13.9 0.6 copy-start.6
  13.9 3.4 %copy-start.4 = (bf16[4,128,1024]{2,1,0:T(8,128)(2,1)S(1)}, bf16[4,128,1024]{2,1,0:T(8,128)(2,1)}, u32[]{:S(2)}) copy-start(bf16[4,128,1024]{2,1,0:T(8,128)(2,1)} %get-tuple-element.42) | copy-start | bytes 3145732 | tf_op jit(solution)/shard_map/cond
  17.2 8.8 %collective-permute-start = (bf16[2048,128]{1,0:T(8,128)(2,1)S(1)}, bf16[2048,128]{1,0:T(8,128)(2,1)S(1)}, u32[]{:S(2)}, u32[]{:S(2)}) collective-permute-start(bf16[2048,128]{1,0:T(8,128)(2,1)S(1)} %decode.3), channel_id=1, source_target_pairs={{0,8},{8,0},{16,24},{24,16},{1,9},{9,1},{17,25},{25,17},{2,10},{10... | collective-permute-start | bytes 1572872 | tf_op jit(solution)/shard_map/cond/branch_1_fun/ppermute | solution.py:22
  18.6 4.5 %copy-start.7 = (f32[1,8192]{1,0:T(1,128)S(1)}, f32[1,8192]{1,0:T(1,128)}, u32[]{:S(2)}) copy-start(f32[1,8192]{1,0:T(1,128)} %copy-done.6) | copy-start | bytes 98308 | tf_op jit(solution)/shard_map/cond
  18.7 41.6 %all-to-all-start = ((bf16[4,192,1024]{2,1,0:T(8,128)(2,1)}), bf16[4,192,1024]{2,1,0:T(8,128)(2,1)}, u32[]{:S(2)}, u32[]{:S(2)}) async-start(bf16[4,192,1024]{2,1,0:T(8,128)(2,1)} %pad_maximum_fusion), calls=%async_computation | async-start | bytes 3145728 | tf_op jit(solution)/shard_map/cond/branch_1_fun/all_to_all | solution.py:352
  23.1 19.5 %copy-start.3 = (f32[524288]{0:T(1024)S(1)}, f32[524288]{0:T(1024)}, u32[]{:S(2)}) copy-start(f32[524288]{0:T(1024)} %get-tuple-element.105) | copy-start | bytes 6291460 | tf_op jit(solution)/shard_map/cond
  26.0 16.7 %copy-start.2 = (f32[524288]{0:T(1024)S(1)}, f32[524288]{0:T(1024)}, u32[]{:S(2)}) copy-start(f32[524288]{0:T(1024)} %get-tuple-element.104) | copy-start | bytes 6291460 | tf_op jit(solution)/shard_map/cond
  26.2 14.4 %collective-permute-start.1 = (bf16[2048,128]{1,0:T(8,128)(2,1)S(1)}, bf16[2048,128]{1,0:T(8,128)(2,1)S(1)}, u32[]{:S(2)}, u32[]{:S(2)}) collective-permute-start(bf16[2048,128]{1,0:T(8,128)(2,1)S(1)} %add_convert_fusion.1), channel_id=1, source_target_pairs={{0,16},{8,24},{16,0},{24,8},{1,17},{9,25},{17,1},{25,9},{2,18},{10... | collective-permute-start | bytes 1572872 | tf_op jit(solution)/shard_map/cond/branch_1_fun/ppermute | solution.py:22
  40.7 2.0 %collective-permute-start.2 = (bf16[2048,128]{1,0:T(8,128)(2,1)S(1)}, bf16[2048,128]{1,0:T(8,128)(2,1)S(1)}, u32[]{:S(2)}, u32[]{:S(2)}) collective-permute-start(bf16[2048,128]{1,0:T(8,128)(2,1)S(1)} %add_convert_fusion.mine_ref), channel_id=1, source_target_pairs={{0,8},{8,0},{16,24},{24,16},{1,9},{9,1},{17,25},{25,17},{2,10},{10... | collective-permute-start | bytes 1572872 | tf_op jit(solution)/shard_map/cond/branch_1_fun/ppermute | solution.py:22
  63.4 9.4 %collective-permute-start.9 = (bf16[5,128,256]{2,1,0:T(8,128)(2,1)S(1)}, bf16[5,128,256]{2,1,0:T(8,128)(2,1)S(1)}, u32[]{:S(2)}, u32[]{:S(2)}) collective-permute-start(bf16[5,128,256]{2,1,0:T(8,128)(2,1)S(1)} %pad_maximum_fusion.2), channel_id=1, source_target_pairs={{0,2},{1,3},{2,0},{3,1},{4,6},{5,7},{6,4},{7,5},{8,10},{9,11},{10,... | collective-permute-start | bytes 983048 | tf_op jit(solution)/shard_map/ppermute | solution.py:22
  65.3 9.2 %collective-permute-start.7 = (bf16[5,128,256]{2,1,0:T(8,128)(2,1)S(1)}, bf16[5,128,256]{2,1,0:T(8,128)(2,1)S(1)}, u32[]{:S(2)}, u32[]{:S(2)}) collective-permute-start(bf16[5,128,256]{2,1,0:T(8,128)(2,1)S(1)} %pad_maximum_fusion.1), channel_id=1, source_target_pairs={{0,1},{1,0},{2,3},{3,2},{4,5},{5,4},{6,7},{7,6},{8,9},{9,8},{10,11... | collective-permute-start | bytes 983048 | tf_op jit(solution)/shard_map/ppermute | solution.py:22
  73.0 7.1 %collective-permute-start.10 = (bf16[4,128,256]{2,1,0:T(8,128)(2,1)S(1)}, bf16[4,128,256]{2,1,0:T(8,128)(2,1)S(1)}, u32[]{:S(2)}, u32[]{:S(2)}) collective-permute-start(bf16[4,128,256]{2,1,0:T(8,128)(2,1)S(1)} %pad_maximum_fusion.4), channel_id=1, source_target_pairs={{0,1},{1,0},{2,3},{3,2},{4,5},{5,4},{6,7},{7,6},{8,9},{9,8},{10,11... | collective-permute-start | bytes 786440 | tf_op jit(solution)/shard_map/ppermute | solution.py:22
  74.7 6.8 %collective-permute-start.8 = (bf16[4,128,256]{2,1,0:T(8,128)(2,1)S(1)}, bf16[4,128,256]{2,1,0:T(8,128)(2,1)S(1)}, u32[]{:S(2)}, u32[]{:S(2)}) collective-permute-start(bf16[4,128,256]{2,1,0:T(8,128)(2,1)S(1)} %pad_maximum_fusion.3), channel_id=1, source_target_pairs={{0,2},{1,3},{2,0},{3,1},{4,6},{5,7},{6,4},{7,5},{8,10},{9,11},{10,... | collective-permute-start | bytes 786440 | tf_op jit(solution)/shard_map/ppermute | solution.py:22
  81.6 7.1 %collective-permute-start.11 = (bf16[128,512]{1,0:T(8,128)(2,1)S(1)}, bf16[128,512]{1,0:T(8,128)(2,1)S(1)}, u32[]{:S(2)}, u32[]{:S(2)}) collective-permute-start(bf16[128,512]{1,0:T(8,128)(2,1)S(1)} %pad_maximum_fusion.8), channel_id=1, source_target_pairs={{0,4},{1,5},{2,6},{3,7},{4,0},{5,1},{6,2},{7,3},{8,12},{9,13},{10,... | collective-permute-start | bytes 393224 | tf_op jit(solution)/shard_map/ppermute | solution.py:22
